TPU v7x, 32 devices: a whole 2x2x4 slice. The times are simulated.
32 devices in a mesh: fsdp: 8 (over z, y), dp: 4 (over x, core).
Axes of the slice: x: 2, y: 2, z: 4, core: 2. Of those that a mesh axis runs over, the one named last changes fastest.
Arguments:
- glu_input: bfloat16 [8192, 3072], P(('fsdp', 'dp')), may hold values from -6 to 6
- frame_counts: int32 [32, 8], P(('fsdp', 'dp')), may hold values from 1 to 128, as said below
- send_rows: int32 [32, 256], P(('fsdp', 'dp')), may hold values from 0 to 256, as said below
- owner_rows: int32 [32, 160], P(('fsdp', 'dp')), may hold values from 0 to 255, as said below
- depth_kernel: float32 [5, 1536], replicated, may hold values from -2.5 to 2.5
- norm_gain: float32 [1536], replicated, may hold values from 0.25 to 1.75
- norm_bias: float32 [1536], replicated, may hold values from -3 to 3
- point_weight: bfloat16 [1536, 1536], P('fsdp'), may hold values from -0.15625 to 0.15625
- cotangent: bfloat16 [5120, 1536], P(('fsdp', 'dp')), may hold values from -6 to 6
Outputs:
- output: bfloat16 [5120, 1536], P(('fsdp', 'dp'))
- input_grad: bfloat16 [8192, 3072], P(('fsdp', 'dp'))
- kernel_grad: float32 [5, 1536], replicated
- norm_grad: float32 [2, 1536], replicated
Inputs may be any that keep to these rules, and one draw needn't show every extreme that they name: `frame_counts`: A device's counts are the lengths of its 8 utterances. A device's total lies from 64 to 256, both reached at every dp index, and the totals of the devices with one dp index sum to 160 times the fsdp axis size. The longest utterance is reached at every dp index. `send_rows`: entry q of a device's list names the local slot whose activation goes to fsdp index q // 32 with the same dp index, as that owner's position q % 32 from this device; the value 256 marks an unused entry. Each live slot is named once, positions for one owner are used from the lowest up, and some device of every dp index fills all 32 positions for every owner. `owner_rows`: entry b names received position p: position p % 32 from fsdp index p // 32 of the same dp index. The 160 entries are distinct and are exactly the positions that senders use for this owner.
All inputs are finite; a program needn't handle non-finite values.
Results may differ from a plain program's by a relative error of at most 0.0085.
Values may be sent and summed in bfloat16 or wider, within the bound.
A program may use at most 64 MiB of HBM per device.

v0:
```python
import math

import jax
import jax.numpy as jnp
from jax import lax
from jax.sharding import PartitionSpec as P

eps = 1e-05


def conv_module(glu_rows, counts, kernel, gain_vec, bias_vec):
    row_count = glu_rows.shape[0]
    chan_count = kernel.shape[1]
    half_width = kernel.shape[0] // 2
    values = glu_rows.astype(jnp.float32)
    mixed_vals = values[:, :chan_count] * jax.nn.sigmoid(values[:, chan_count:])
    utter_ends = jnp.cumsum(counts)
    position = jnp.arange(row_count, dtype=jnp.int32)
    segment = jnp.sum((position[:, None] >= utter_ends[None, :]).astype(jnp.int32), axis=1)
    is_live = position < utter_ends[-1]
    mixed_vals = jnp.where(is_live[:, None], mixed_vals, 0.0)
    padded = jnp.pad(mixed_vals, ((half_width, half_width), (0, 0)))
    labels = jnp.pad(segment, (half_width, half_width), constant_values=-1)
    conv_out = jnp.zeros((row_count, chan_count), jnp.float32)
    for offset in range(2 * half_width + 1):
        same_utt = labels[offset : offset + row_count] == segment
        conv_out = (
            conv_out
            + jnp.where(same_utt[:, None], padded[offset : offset + row_count], 0.0)
            * kernel[offset]
        )
    center = jnp.mean(conv_out, axis=1, keepdims=True)
    spread = jnp.mean(jnp.square(conv_out - center), axis=1, keepdims=True)
    normed = (conv_out - center) * lax.rsqrt(spread + eps) * gain_vec + bias_vec
    activated = normed * jax.nn.sigmoid(normed)
    return jnp.where(is_live[:, None], activated, 0.0)


def per_device(
    glu_input,
    frame_counts,
    send_rows,
    owner_rows,
    depth_kernel,
    norm_gain,
    norm_bias,
    point_weight,
    cotangent,
):
    counts = frame_counts[0]
    send_slot = send_rows[0]
    owner_slot = owner_rows[0]
    row_count = glu_input.shape[0]
    out_count = point_weight.shape[1]

    def local_pass(glu_rows, kernel, gain_vec, bias_vec):
        return conv_module(glu_rows, counts, kernel, gain_vec, bias_vec)

    activated, pullback = jax.vjp(local_pass, glu_input, depth_kernel, norm_gain, norm_bias)
    activations = activated.astype(jnp.bfloat16)
    produced = jnp.dot(
        activations,
        lax.all_gather(point_weight, "fsdp", axis=0, tiled=True),
        preferred_element_type=jnp.float32,
    ).astype(jnp.bfloat16)
    outgoing = jnp.concatenate([produced, jnp.zeros((1, out_count), jnp.bfloat16)], axis=0)[
        send_slot
    ]
    arrived = lax.all_to_all(outgoing, "fsdp", split_axis=0, concat_axis=0, tiled=True)
    output = arrived[owner_slot]
    parked = jnp.zeros((row_count, out_count), jnp.bfloat16).at[owner_slot].set(cotangent)
    returned = lax.all_to_all(parked, "fsdp", split_axis=0, concat_axis=0, tiled=True)
    home_rows = (
        jnp.zeros((row_count + 1, out_count), jnp.bfloat16).at[send_slot].set(returned)[:row_count]
    )
    grad_acts = lax.dot_general(
        home_rows,
        lax.all_gather(point_weight, "fsdp", axis=0, tiled=True),
        (((1,), (1,)), ((), ())),
        preferred_element_type=jnp.float32,
    ).astype(jnp.bfloat16)
    input_grad, kernel_part, gain_part, bias_part = pullback(grad_acts.astype(jnp.float32))
    totals = lax.psum((kernel_part, jnp.stack([gain_part, bias_part])), ("fsdp", "dp"))
    frame_total = owner_slot.shape[0] * lax.axis_size("fsdp") * lax.axis_size("dp")
    grad_scale = 1.0 / math.sqrt(frame_total)
    return (output, input_grad, totals[0] * grad_scale, totals[1] * grad_scale)


def solution(mesh):
    in_specs = (
        P(("fsdp", "dp"), None),
        P(("fsdp", "dp"), None),
        P(("fsdp", "dp"), None),
        P(("fsdp", "dp"), None),
        P(),
        P(),
        P(),
        P("fsdp", None),
        P(("fsdp", "dp"), None),
    )
    out_specs = (P(("fsdp", "dp"), None), P(("fsdp", "dp"), None), P(), P())
    return jax.shard_map(
        per_device, mesh=mesh, in_specs=in_specs, out_specs=out_specs, check_vma=False
    )
```

profile of v0, /device:TPU:0, one launch (start us, length us, event | category | flops | bytes accessed | tf_op | source)
XLA Modules:
  0.0 183.9 jit_solution(5087588050780621901)
XLA Ops:
  7.2 0.0 all-gather.2.cloned.1.call-start
  7.2 0.7 all-gather.2.cloned.1.call-update
  7.9 0.7 compare_select_fusion
  8.6 2.9 %scatter_custom_fusion = bf16[256,1536]{1,0:T(8,128)(2,1)} fusion(s32[160]{0:T(256)S(1)} %bitcast.19, bf16[160,1536]{1,0:T(8,128)(2,1)} %param.17, bf16[]{:T(256)} %constant.43.clone.1), kind=kCustom, calls=%fused_computation.58 | custom fusion | bytes 786944 | tf_op jit(solution)/shard_map/scatter | solution.py:71
  11.5 7.3 %all-to-all-start.1 = ((bf16[8,32,1536]{2,1,0:T(8,128)(2,1)}), bf16[8,32,1536]{2,1,0:T(8,128)(2,1)}, u32[]{:S(2)}, u32[]{:S(2)}) async-start(bf16[8,32,1536]{2,1,0:T(8,128)(2,1)} %bitcast.9), calls=%async_computation.1 | async-start | bytes 1572864 | tf_op jit(solution)/shard_map/all_to_all | solution.py:72
  18.7 0.0 copy-start.7
  18.8 1.9 %convert_element_type.24 = f32[256,3072]{1,0:T(8,128)S(1)} convert(bf16[256,3072]{1,0:T(8,128)(2,1)} %param.9) | non-fusion elementwise | flops 786432 | bytes 4718592 | tf_op jit(solution)/shard_map/jvp()/convert_element_type | solution.py:15
  20.6 0.0 copy-start
  20.6 0.0 copy-done.9
  20.6 0.2 reduce-window.4
  20.8 0.8 slice.55
  21.6 0.7 iota_compare_fusion.1
  22.3 0.1 convert_reduce_fusion
  22.4 0.0 copy-done.7
  22.4 0.4 multiply_select_fusion.4
  22.9 0.0 copy-done
  22.9 0.0 copy-start.2
  22.9 0.3 copy-done.5
  23.2 0.1 slice_reduce_fusion.4
  23.3 0.1 fusion.21
  23.4 1.6 fusion.30
  25.0 0.0 copy-done.2
  25.0 0.0 copy-start.6
  25.0 0.0 copy-start.8
  25.0 0.3 multiply_reduce_fusion.7
  25.4 30.5 %all-to-all-done.1 = bf16[8,32,1536]{2,1,0:T(8,128)(2,1)} async-done(((bf16[8,32,1536]{2,1,0:T(8,128)(2,1)}), bf16[8,32,1536]{2,1,0:T(8,128)(2,1)}, u32[]{:S(2)}, u32[]{:S(2)}) %all-to-all-start.1) | async-done | bytes 786464 | tf_op jit(solution)/shard_map/all_to_all | solution.py:72
  55.9 3.4 %scatter_custom_fusion.1 = bf16[257,1536]{1,0:T(8,128)(2,1)} fusion(s32[256]{0:T(256)S(1)} %bitcast.18, bf16[256,1536]{1,0:T(8,128)(2,1)} %bitcast.10, bf16[]{:T(256)} %constant.43.clone.1), kind=kCustom, calls=%fused_computation.56 | custom fusion | bytes 790016 | tf_op jit(solution)/shard_map/scatter | solution.py:74
  59.2 47.4 %all-gather.2.cloned.1.call-done = bf16[1536,1536]{1,0:T(8,128)(2,1)} async-done(((bf16[192,1536]{1,0:T(8,128)(2,1)}), bf16[1536,1536]{1,0:T(8,128)(2,1)}) %all-gather.2.cloned.1.call-update) | async-done | bytes 4718608 | tf_op jit(solution)/shard_map/all_gather | solution.py:63
  106.7 0.0 copy-done.6
  106.7 3.9 %convolution_convert_fusion.1 = bf16[256,1536]{1,0:T(8,128)(2,1)S(1)} fusion(bf16[1536,1536]{1,0:T(8,128)(2,1)} %all-gather.2.cloned.1.call-done, f32[256,1536]{1,0:T(8,128)S(1)} %get-tuple-element.24, f32[1536]{0:T(1024)S(1)} %copy-done.8, f32[1536]{0:T(1024)S(1)} %copy-done.6, f32[256]{0:T(256)S(1)} %fusion.25, f32[256]{0:T(256)S(1)} %broadcast_multiply_fusion.3, ...), kind=kOutput, calls=%fused_computation.8 | convolution fusion | flops 1212284928 | bytes 7092480 | tf_op jit(solution)/shard_map/dot_general | solution.py:61
  110.6 0.1 concatenate.3
  110.6 2.2 %gather_fusion = bf16[256,1536]{1,0:T(8,128)(2,1)} fusion(bf16[257,1536]{1,0:T(8,128)(2,1)S(1)} %concatenate.3, s32[1024]{0:T(1024)S(1)} %pad_clamp_fusion.1), kind=kCustom, calls=%fused_computation | custom fusion | bytes 1573888 | tf_op jit(solution)/shard_map/gather | solution.py:66
  112.8 3.9 %all-to-all-start = ((bf16[8,32,1536]{2,1,0:T(8,128)(2,1)}), bf16[8,32,1536]{2,1,0:T(8,128)(2,1)S(1)}, u32[]{:S(2)}, u32[]{:S(2)}) async-start(bf16[8,32,1536]{2,1,0:T(8,128)(2,1)} %bitcast.16), calls=%async_computation | async-start | bytes 1572864 | tf_op jit(solution)/shard_map/all_to_all | solution.py:69
  116.7 0.0 copy-done.4
  116.7 4.7 %multiply_reduce_fusion = (f32[1536]{0:T(1024)S(1)}, f32[256]{0:T(256)S(1)}, f32[256]{0:T(256)S(1)}, f32[1536]{0:T(1024)S(1)}, f32[256,1536]{1,0:T(8,128)S(1)}) fusion(f32[256,1536]{1,0:T(8,128)S(1)} %get-tuple-element.24, f32[256]{0:T(256)S(1)} %fusion.25, f32[256]{0:T(256)S(1)} %broadcast_multiply_fusion.3, f32[1536]{0:T(1024)S(1)} %copy-done.6, ...), kind=kOutput, calls=%fused_computation.23 | convolution fusion | flops 1217393152 | bytes 8684032 | tf_op jit(solution)/shard_map/dot_general | solution.py:76
  121.4 0.3 multiply_reduce_fusion.8
  121.7 1.1 copy-done.3
  122.8 2.3 %multiply_reduce_fusion.5 = (f32[1536]{0:T(1024)S(1)}, f32[1536]{0:T(1024)S(1)}, f32[1536]{0:T(1024)S(1)}, f32[1536]{0:T(1024)S(1)}, f32[1536]{0:T(1024)S(1)}, /*index=5*/f32[256,1536]{1,0:T(8,128)S(1)}) fusion(f32[256,1536]{1,0:T(8,128)S(1)} %copy-done.3, pred[256]{0:T(512)(128)(4,1)S(1)} %get-tuple-element.33, pred[256]{0:T(512)(128)(4,1)S(1)} %get-tuple-element.30, ...), kind=kLoop, calls=%fused_computation.28 | loop fusion | flops 7856640 | bytes 6333440 | tf_op jit(solution)/shard_map/transpose(jvp())/reduce_sum | solution.py:29
  125.2 0.7 multiply_select_fusion.3
  125.9 1.1 copy-done.1
  127.0 2.5 %fusion.4 = (f32[256,1536]{1,0:T(8,128)}, f32[256,1536]{1,0:T(8,128)S(1)}) fusion(f32[256,3072]{1,0:T(8,128)S(1)} %copy-done.1, f32[256,1536]{1,0:T(8,128)S(1)} %get-tuple-element.26, f32[256,1536]{1,0:T(8,128)S(1)} %get-tuple-element.27, f32[256,1536]{1,0:T(8,128)S(1)} %get-tuple-element.28, f32[256,1536]{1,0:T(8,128)S(1)} %get-tuple-element.29, ...), kind=kLoop, calls=%fused_computation.13 | loop fusion | flops 4718592 | bytes 14156032 | tf_op jit(solution)/shard_map/transpose(jvp())/mul | solution.py:16
  129.6 0.4 fusion.28
  130.2 41.2 %all-reduce.15 = (f32[5,1536]{1,0:T(8,128)S(1)}, f32[2,1536]{1,0:T(2,128)S(1)}) all-reduce(f32[5,1536]{1,0:T(8,128)S(1)} %pad_add_fusion.4, f32[2,1536]{1,0:T(2,128)S(1)} %pad_maximum_fusion), channel_id=1, replica_groups=mesh['fsdp'=8,'dp'=4] {'fsdp','dp'}, use_global_device_ids=true, to_apply=%region_14.15 | all-reduce | flops 10752 | bytes 86016 | tf_op jit(solution)/shard_map/psum | solution.py:83
  171.3 2.8 %add_convert_fusion = bf16[256,3072]{1,0:T(8,128)(2,1)} fusion(f32[256,1536]{1,0:T(8,128)S(1)} %fusion.28, f32[256,1536]{1,0:T(8,128)} %get-tuple-element.21), kind=kLoop, calls=%fused_computation.4 | loop fusion | flops 1572864 | bytes 4718592 | tf_op jit(solution)/shard_map/transpose(jvp())/convert_element_type | solution.py:15
  174.1 0.6 broadcast_multiply_fusion.2
  174.7 0.6 broadcast_multiply_fusion.1
  175.3 0.0 all-to-all-done
  175.3 1.8 gather_fusion.1
  (22 shorter events, 0.2 us)
Async XLA Ops:
  7.2 99.5 %all-gather.2.cloned.1.call-start = ((), (), s32[]{:S(2)}) async-start(), calls=%async_computation.2 | async-start | bytes 5308416 | tf_op jit(solution)/shard_map/all_gather | solution.py:63
  11.5 44.4 %all-to-all-start.1 = ((bf16[8,32,1536]{2,1,0:T(8,128)(2,1)}), bf16[8,32,1536]{2,1,0:T(8,128)(2,1)}, u32[]{:S(2)}, u32[]{:S(2)}) async-start(bf16[8,32,1536]{2,1,0:T(8,128)(2,1)} %bitcast.9), calls=%async_computation.1 | async-start | bytes 1572864 | tf_op jit(solution)/shard_map/all_to_all | solution.py:72
  18.7 1.9 %copy-start.9 = (s32[1,8]{1,0:T(1,128)S(1)}, s32[1,8]{1,0:T(1,128)}, u32[]{:S(2)}) copy-start(s32[1,8]{1,0:T(1,128)} %param.10) | copy-start | bytes 100
  18.7 3.7 %copy-start.7 = (s32[1,256]{1,0:T(1,128)S(1)}, s32[1,256]{1,0:T(1,128)}, u32[]{:S(2)}) copy-start(s32[1,256]{1,0:T(1,128)} %param.11) | copy-start | bytes 3076
  20.6 2.2 %copy-start = (f32[256,3072]{1,0:T(8,128)}, f32[256,3072]{1,0:T(8,128)S(1)}, u32[]{:S(2)}) copy-start(f32[256,3072]{1,0:T(8,128)S(1)} %convert_element_type.24) | copy-start | bytes 9437188
  22.4 0.8 copy-start.5
  22.9 2.1 %copy-start.2 = (f32[256,1536]{1,0:T(8,128)}, f32[256,1536]{1,0:T(8,128)S(1)}, u32[]{:S(2)}) copy-start(f32[256,1536]{1,0:T(8,128)S(1)} %multiply_select_fusion.4) | copy-start | bytes 4718596
  25.0 81.7 %copy-start.6 = (f32[1536]{0:T(1024)S(1)}, f32[1536]{0:T(1024)}, u32[]{:S(2)}) copy-start(f32[1536]{0:T(1024)} %param.14) | copy-start | bytes 18436
  25.0 81.6 %copy-start.8 = (f32[1536]{0:T(1024)S(1)}, f32[1536]{0:T(1024)}, u32[]{:S(2)}) copy-start(f32[1536]{0:T(1024)} %param.15) | copy-start | bytes 18436
  112.8 3.9 %copy-start.4 = (bf16[257,1536]{1,0:T(8,128)(2,1)S(1)}, bf16[257,1536]{1,0:T(8,128)(2,1)}, u32[]{:S(2)}) copy-start(bf16[257,1536]{1,0:T(8,128)(2,1)} %scatter_custom_fusion.1) | copy-start | bytes 2368516
  112.8 62.5 %all-to-all-start = ((bf16[8,32,1536]{2,1,0:T(8,128)(2,1)}), bf16[8,32,1536]{2,1,0:T(8,128)(2,1)S(1)}, u32[]{:S(2)}, u32[]{:S(2)}) async-start(bf16[8,32,1536]{2,1,0:T(8,128)(2,1)} %bitcast.16), calls=%async_computation | async-start | bytes 1572864 | tf_op jit(solution)/shard_map/all_to_all | solution.py:69
  121.4 1.4 copy-start.3
  125.1 1.9 %copy-start.1 = (f32[256,3072]{1,0:T(8,128)S(1)}, f32[256,3072]{1,0:T(8,128)}, u32[]{:S(2)}) copy-start(f32[256,3072]{1,0:T(8,128)} %copy-done) | copy-start | bytes 9437188
Sparse Core Ops, SparseCore 0:
  10.2 96.4 all-gather.1
where the time goes:
time: 185 us; the launch traced here: 184 us
  waiting for transfers between devices  78.6 us (42%)
  blocking collectives  41.2 us (22%)
  other arithmetic  16.3 us (9%)
  between operations  14.3 us (8%)
  local copies, waits for them, and re-layouts  13.8 us (7%)
  starting transfers between devices  11.2 us (6%)
  matrix products  8.56 us (5%)
    all_gather x1, waiting for transfers between devices, per_device(): lax.all_gather(point_weight, 'fsdp', axis=0, tiled=True)  47.4 us
    psum x1, blocking collectives, per_device(): lax.psum((kernel_part, jnp.stack([gain_part, bias_part])), ('fsdp', 'dp'))  41.2 us
    all_to_all x1, waiting for transfers between devices, per_device(): lax.all_to_all(parked, 'fsdp', split_axis=0, concat_axis=0, tiled=True)  30.5 us
    all_to_all x1, starting transfers between devices, per_device(): lax.all_to_all(parked, 'fsdp', split_axis=0, concat_axis=0, tiled=True)  7.28 us
    dot_general x1, matrix products, per_device(): lax.dot_general(home_rows, lax.all_gather(point_weight, 'fsdp', axis=0, t...  4.67 us
    convert_element_type x2, other arithmetic, conv_module(): values = glu_rows.astype(jnp.float32)  4.62 us
    dot_general x1, matrix products, per_device(): jnp.dot(activations, lax.all_gather(point_weight, 'fsdp', axis=0, tiled=T...  3.89 us
    all_to_all x1, starting transfers between devices, per_device(): lax.all_to_all(outgoing, 'fsdp', split_axis=0, concat_axis=0, tiled=True)  3.86 us
  transfers between devices with their start and end apart: 3, of which 2 were waited for; matrix products, arithmetic and copies ran while one was open for 15% of the time, Pallas kernels for 0%

commit v1 on v0

--- a/solution.py
+++ b/solution.py
@@ -1,11 +1,480 @@
+import functools
 import math
 
 import jax
 import jax.numpy as jnp
 from jax import lax
+from jax.experimental import pallas as pl
+from jax.experimental.pallas import tpu as pltpu
 from jax.sharding import PartitionSpec as P
 
 eps = 1e-05
+LANES = 128
+F32 = jnp.float32
+BF16 = jnp.bfloat16
+
+
+def fused_kernel(
+    n_fsdp,
+    n_dp,
+    counts_ref,
+    glu_ref,
+    send_ref,
+    owner_ref,
+    taps_ref,
+    gain_ref,
+    bias_ref,
+    weight_ref,
+    cot_ref,
+    out_ref,
+    igrad_ref,
+    kgrad_ref,
+    ngrad_ref,
+    w_buf,
+    parked,
+    returned,
+    home,
+    acts,
+    outgoing,
+    arrived,
+    mixed_buf,
+    conv_buf,
+    grad_buf,
+    back_buf,
+    dp_in,
+    rs_src,
+    rs_in,
+    full,
+    w_send,
+    w_recv,
+    cot_send,
+    cot_recv,
+    act_send,
+    act_recv,
+    dp_send,
+    dp_recv,
+    rs_send,
+    rs_recv,
+    ag_send,
+    ag_recv,
+):
+    f = lax.axis_index("fsdp")
+    d = lax.axis_index("dp")
+    rows = glu_ref.shape[0]
+    chans = taps_ref.shape[1]
+    taps = taps_ref.shape[0]
+    half = taps // 2
+    panel = weight_ref.shape[0]
+    cols = weight_ref.shape[1]
+    piece = cols // n_dp
+    slots = rows // n_fsdp
+    owned = cot_ref.shape[0]
+    utts = counts_ref.shape[1]
+    chunk = full.shape[1] // n_fsdp
+    n_chunks = chans // LANES
+
+    y_peer = f + 1 - 2 * (f % 2)
+    x_peer = (d + n_dp // 2) % n_dp
+    core_peer = d + 1 - 2 * (d % 2)
+
+    barrier = pltpu.get_barrier_semaphore()
+    for k in range(1, n_fsdp):
+        pl.semaphore_signal(barrier, inc=1, device_id={"fsdp": (f + k) % n_fsdp, "dp": d})
+    for k in range(1, n_dp):
+        pl.semaphore_signal(barrier, inc=1, device_id={"fsdp": f, "dp": (d + k) % n_dp})
+    pl.semaphore_wait(barrier, n_fsdp + n_dp - 2)
+
+    def rows_of(p, size):
+        return pl.ds(pl.multiple_of(p * size, size), size)
+
+    def piece_of(p, q):
+        return w_buf.at[rows_of(p, panel), rows_of(q, piece)]
+
+    pending = []
+
+    def send_piece(src, p, q, kind, slot, target):
+        copy = pltpu.make_async_remote_copy(
+            src_ref=src,
+            dst_ref=piece_of(p, q),
+            send_sem=w_send.at[kind, slot],
+            recv_sem=w_recv.at[p, q],
+            device_id=target,
+        )
+        copy.start()
+        pending.append(copy)
+
+    def wait_piece(p, q):
+        pltpu.make_async_remote_copy(
+            src_ref=piece_of(p, q),
+            dst_ref=piece_of(p, q),
+            send_sem=w_send.at[0, 0],
+            recv_sem=w_recv.at[p, q],
+            device_id={"fsdp": f, "dp": core_peer},
+        ).wait_recv()
+
+    own_piece = weight_ref.at[:, rows_of(d, piece)]
+    z_steps = range(1, n_fsdp // 2)
+    for k in z_steps:
+        send_piece(own_piece, f, d, 0, k, {"fsdp": (f + 2 * k) % n_fsdp, "dp": d})
+    send_piece(own_piece, f, d, 1, 0, {"fsdp": y_peer, "dp": d})
+
+    def exchange(src, dst, send_sem, recv_sem):
+        copies = []
+        for k in range(1, n_fsdp):
+            target = (f + k) % n_fsdp
+            copy = pltpu.make_async_remote_copy(
+                src_ref=src.at[rows_of(target, slots)],
+                dst_ref=dst.at[rows_of(f, slots)],
+                send_sem=send_sem.at[target],
+                recv_sem=recv_sem.at[f],
+                device_id={"fsdp": target, "dp": d},
+            )
+            copy.start()
+            copies.append(copy)
+        dst[rows_of(f, slots), :] = src[rows_of(f, slots), :]
+        return copies
+
+    def finish_exchange(copies, src, dst, send_sem, recv_sem):
+        for k in range(1, n_fsdp):
+            source = (f + k) % n_fsdp
+            pltpu.make_async_remote_copy(
+                src_ref=src.at[rows_of(source, slots)],
+                dst_ref=dst.at[rows_of(source, slots)],
+                send_sem=send_sem.at[source],
+                recv_sem=recv_sem.at[source],
+                device_id={"fsdp": source, "dp": d},
+            ).wait_recv()
+        pending.extend(copies)
+
+    park = (
+        lax.broadcasted_iota(jnp.int32, (rows, owned), 0) == owner_ref[...]
+    ).astype(F32).astype(BF16)
+    parked[...] = jnp.dot(park, cot_ref[...], preferred_element_type=F32).astype(BF16)
+    cot_copies = exchange(parked, returned, cot_send, cot_recv)
+
+    w_buf[rows_of(f, panel), :] = weight_ref[...]
+
+    ends = []
+    total = jnp.int32(0)
+    for u in range(utts):
+        total = total + counts_ref[0, u]
+        ends.append(total)
+    pos = lax.broadcasted_iota(jnp.int32, (rows, LANES), 0)
+
+    def segment(at):
+        seg = jnp.zeros((rows, LANES), jnp.int32)
+        for end in ends:
+            seg = seg + (at >= end).astype(jnp.int32)
+        return seg
+
+    own_seg = segment(pos)
+    live = pos < total
+    live_f = live.astype(F32)
+    masks = []
+    for j in range(taps):
+        at = pos + (j - half)
+        same = (segment(at) == own_seg) & live & (at >= 0) & (at < rows)
+        masks.append(same.astype(F32))
+
+    def lanes_of(i):
+        return pl.ds(pl.multiple_of(i * LANES, LANES), LANES)
+
+    def shifted(x, offset):
+        return x if offset == 0 else pltpu.roll(x, (-offset) % rows, 0)
+
+    def conv_step(i, acc):
+        a = glu_ref[:, lanes_of(i)].astype(F32)
+        b = glu_ref[:, pl.ds(pl.multiple_of(chans + i * LANES, LANES), LANES)].astype(F32)
+        mixed = a * jax.nn.sigmoid(b) * live_f
+        mixed_buf[:, lanes_of(i)] = mixed
+        conv = jnp.zeros((rows, LANES), F32)
+        for j in range(taps):
+            conv = conv + masks[j] * shifted(mixed, j - half) * taps_ref[j : j + 1, lanes_of(i)]
+        conv_buf[:, lanes_of(i)] = conv
+        return acc + conv
+
+    zero_acc = jnp.zeros((rows, LANES), F32)
+    acc = lax.fori_loop(0, n_chunks, conv_step, zero_acc)
+    mean = jnp.sum(acc, axis=1, keepdims=True) * (1.0 / chans)
+
+    for k in z_steps:
+        p = (f + 2 * k) % n_fsdp
+        wait_piece(p, d)
+        src = piece_of(p, d)
+        send_piece(src, p, d, 1, k, {"fsdp": y_peer, "dp": d})
+        send_piece(src, p, d, 2, k, {"fsdp": f, "dp": x_peer})
+        send_piece(src, p, d, 3, k, {"fsdp": f, "dp": core_peer})
+
+    def var_step(i, acc):
+        diff = conv_buf[:, lanes_of(i)] - mean
+        return acc + diff * diff
+
+    acc = lax.fori_loop(0, n_chunks, var_step, zero_acc)
+    rstd = lax.rsqrt(jnp.sum(acc, axis=1, keepdims=True) * (1.0 / chans) + eps)
+
+    def act_step(i, carry):
+        xhat = (conv_buf[:, lanes_of(i)] - mean) * rstd
+        conv_buf[:, lanes_of(i)] = xhat
+        normed = xhat * gain_ref[:, lanes_of(i)] + bias_ref[:, lanes_of(i)]
+        acts[:, lanes_of(i)] = (normed * jax.nn.sigmoid(normed) * live_f).astype(BF16)
+        return carry
+
+    lax.fori_loop(0, n_chunks, act_step, 0)
+    pick = (
+        lax.broadcasted_iota(jnp.int32, (rows, rows), 0) == send_ref[...]
+    ).astype(F32).astype(BF16)
+    outgoing[...] = lax.dot_general(
+        pick, acts[...], (((0,), (0,)), ((), ())), preferred_element_type=F32
+    ).astype(BF16)
+
+    for k in range(n_fsdp // 2):
+        p = (y_peer + 2 * k) % n_fsdp
+        wait_piece(p, d)
+        src = piece_of(p, d)
+        send_piece(src, p, d, 2, n_fsdp // 2 + k, {"fsdp": f, "dp": x_peer})
+        send_piece(src, p, d, 3, n_fsdp // 2 + k, {"fsdp": f, "dp": core_peer})
+
+    act_copies = exchange(outgoing, arrived, act_send, act_recv)
+
+    order = [(f + 2 * k) % n_fsdp for k in z_steps]
+    order += [(y_peer + 2 * k) % n_fsdp for k in range(n_fsdp // 2)]
+    for k, p in enumerate(order):
+        wait_piece(p, x_peer)
+        send_piece(piece_of(p, x_peer), p, x_peer, 4, k, {"fsdp": f, "dp": core_peer})
+
+    finish_exchange(cot_copies, parked, returned, cot_send, cot_recv)
+    home[...] = jnp.dot(pick, returned[...], preferred_element_type=F32).astype(BF16)
+
+    for p in order:
+        wait_piece(p, core_peer)
+        wait_piece(p, (core_peer + n_dp // 2) % n_dp)
+
+    wide = 2 * LANES
+
+    def back_step(i, carry):
+        at = pl.ds(pl.multiple_of(i * wide, wide), wide)
+        back_buf[:, at] = lax.dot_general(
+            home[...], w_buf[at, :], (((1,), (1,)), ((), ())), preferred_element_type=F32
+        ).astype(BF16)
+        return carry
+
+    lax.fori_loop(0, chans // wide, back_step, 0)
+
+    part = dp_in.at[d]
+    dp_in[d] = jnp.zeros(dp_in.shape[1:], F32)
+
+    def norm_step(i, sums):
+        xhat = conv_buf[:, lanes_of(i)]
+        gain = gain_ref[:, lanes_of(i)]
+        normed = xhat * gain + bias_ref[:, lanes_of(i)]
+        s = jax.nn.sigmoid(normed)
+        g = back_buf[:, lanes_of(i)].astype(F32) * live_f
+        dn = g * (s + normed * s * (1.0 - s))
+        dnx = dn * xhat
+        part[taps : taps + 1, lanes_of(i)] = jnp.sum(dnx, axis=0, keepdims=True)
+        part[taps + 1 : taps + 2, lanes_of(i)] = jnp.sum(dn, axis=0, keepdims=True)
+        grad_buf[:, lanes_of(i)] = dn * gain
+        return sums[0] + dn * gain, sums[1] + dnx * gain
+
+    first, second = lax.fori_loop(0, n_chunks, norm_step, (zero_acc, zero_acc))
+    first = jnp.sum(first, axis=1, keepdims=True) * (1.0 / chans)
+    second = jnp.sum(second, axis=1, keepdims=True) * (1.0 / chans)
+
+    def grad_step(i, carry):
+        dconv = rstd * (grad_buf[:, lanes_of(i)] - first - conv_buf[:, lanes_of(i)] * second)
+        mixed = mixed_buf[:, lanes_of(i)]
+        dmixed = jnp.zeros((rows, LANES), F32)
+        for j in range(taps):
+            moved = masks[taps - 1 - j] * shifted(dconv, half - j)
+            part[j : j + 1, lanes_of(i)] = jnp.sum(mixed * moved, axis=0, keepdims=True)
+            dmixed = dmixed + moved * taps_ref[j : j + 1, lanes_of(i)]
+        a = glu_ref[:, lanes_of(i)].astype(F32)
+        right = pl.ds(pl.multiple_of(chans + i * LANES, LANES), LANES)
+        sb = jax.nn.sigmoid(glu_ref[:, right].astype(F32))
+        ds = dmixed * sb
+        igrad_ref[:, lanes_of(i)] = ds.astype(BF16)
+        igrad_ref[:, right] = (ds * a * (1.0 - sb)).astype(BF16)
+        return carry
+
+    lax.fori_loop(0, n_chunks, grad_step, 0)
+
+    dp_copies = []
+    for k in range(1, n_dp):
+        target = (d + k) % n_dp
+        copy = pltpu.make_async_remote_copy(
+            src_ref=dp_in.at[d],
+            dst_ref=dp_in.at[d],
+            send_sem=dp_send.at[k],
+            recv_sem=dp_recv.at[d],
+            device_id={"fsdp": f, "dp": target},
+        )
+        copy.start()
+        dp_copies.append(copy)
+
+    finish_exchange(act_copies, outgoing, arrived, act_send, act_recv)
+    outgoing_rows = lax.dot_general(
+        park, arrived[...], (((0,), (0,)), ((), ())), preferred_element_type=F32
+    ).astype(BF16)
+    acts[0:owned, :] = outgoing_rows
+
+    for k in range(1, n_dp):
+        source = (d + k) % n_dp
+        pltpu.make_async_remote_copy(
+            src_ref=dp_in.at[source],
+            dst_ref=dp_in.at[source],
+            send_sem=dp_send.at[k],
+            recv_sem=dp_recv.at[source],
+            device_id={"fsdp": f, "dp": source},
+        ).wait_recv()
+    pending.extend(dp_copies)
+    summed = dp_in[0]
+    for q in range(1, n_dp):
+        summed = summed + dp_in[q]
+    rs_src[...] = summed
+
+    rs_copies = []
+    for k in range(1, n_fsdp):
+        target = (f + k) % n_fsdp
+        copy = pltpu.make_async_remote_copy(
+            src_ref=rs_src.at[:, rows_of(target, chunk)],
+            dst_ref=rs_in.at[f],
+            send_sem=rs_send.at[target],
+            recv_sem=rs_recv.at[f],
+            device_id={"fsdp": target, "dp": d},
+        )
+        copy.start()
+        rs_copies.append(copy)
+    rs_in[f] = rs_src[:, rows_of(f, chunk)]
+
+    def out_step(i, carry):
+        at = pl.ds(pl.multiple_of(i * wide, wide), wide)
+        out_ref[:, at] = jnp.dot(
+            acts[0:owned, :], w_buf[:, at], preferred_element_type=F32
+        ).astype(BF16)
+        return carry
+
+    lax.fori_loop(0, cols // wide, out_step, 0)
+
+    for k in range(1, n_fsdp):
+        source = (f + k) % n_fsdp
+        pltpu.make_async_remote_copy(
+            src_ref=rs_src.at[:, rows_of(source, chunk)],
+            dst_ref=rs_in.at[source],
+            send_sem=rs_send.at[source],
+            recv_sem=rs_recv.at[source],
+            device_id={"fsdp": source, "dp": d},
+        ).wait_recv()
+    pending.extend(rs_copies)
+    reduced = rs_in[0]
+    for q in range(1, n_fsdp):
+        reduced = reduced + rs_in[q]
+    scale = 1.0 / math.sqrt(owned * n_fsdp * n_dp)
+    full[:, rows_of(f, chunk)] = reduced * scale
+    ag_copies = []
+    for k in range(1, n_fsdp):
+        target = (f + k) % n_fsdp
+        copy = pltpu.make_async_remote_copy(
+            src_ref=full.at[:, rows_of(f, chunk)],
+            dst_ref=full.at[:, rows_of(f, chunk)],
+            send_sem=ag_send.at[target],
+            recv_sem=ag_recv.at[f],
+            device_id={"fsdp": target, "dp": d},
+        )
+        copy.start()
+        ag_copies.append(copy)
+    for k in range(1, n_fsdp):
+        source = (f + k) % n_fsdp
+        pltpu.make_async_remote_copy(
+            src_ref=full.at[:, rows_of(source, chunk)],
+            dst_ref=full.at[:, rows_of(source, chunk)],
+            send_sem=ag_send.at[source],
+            recv_sem=ag_recv.at[source],
+            device_id={"fsdp": source, "dp": d},
+        ).wait_recv()
+    pending.extend(ag_copies)
+    kgrad_ref[...] = full[0:taps, 0:chans]
+    ngrad_ref[...] = full[taps : taps + 2, 0:chans]
+    for copy in pending:
+        copy.wait_send()
+
+
+def fused_call(
+    n_fsdp,
+    n_dp,
+    glu_input,
+    frame_counts,
+    send_rows,
+    owner_rows,
+    depth_kernel,
+    norm_gain,
+    norm_bias,
+    point_weight,
+    cotangent,
+):
+    rows, glu_cols = glu_input.shape
+    taps, chans = depth_kernel.shape
+    panel, cols = point_weight.shape
+    owned = cotangent.shape[0]
+    sum_rows = -(-(taps + 2) // 8) * 8
+    chunk = -(-chans // (n_fsdp * LANES)) * LANES
+    padded = chunk * n_fsdp
+    vmem = pl.BlockSpec(memory_space=pltpu.VMEM)
+    smem = pl.BlockSpec(memory_space=pltpu.SMEM)
+    dma = pltpu.SemaphoreType.DMA
+    return pl.pallas_call(
+        functools.partial(fused_kernel, n_fsdp, n_dp),
+        out_shape=(
+            jax.ShapeDtypeStruct((owned, cols), BF16),
+            jax.ShapeDtypeStruct((rows, glu_cols), BF16),
+            jax.ShapeDtypeStruct((taps, chans), F32),
+            jax.ShapeDtypeStruct((2, chans), F32),
+        ),
+        in_specs=[smem] + [vmem] * 8,
+        out_specs=(vmem,) * 4,
+        scratch_shapes=[
+            pltpu.VMEM((chans, cols), BF16),
+            pltpu.VMEM((rows, cols), BF16),
+            pltpu.VMEM((rows, cols), BF16),
+            pltpu.VMEM((rows, cols), BF16),
+            pltpu.VMEM((rows, chans), BF16),
+            pltpu.VMEM((rows, chans), BF16),
+            pltpu.VMEM((rows, chans), BF16),
+            pltpu.VMEM((rows, chans), F32),
+            pltpu.VMEM((rows, chans), F32),
+            pltpu.VMEM((rows, chans), F32),
+            pltpu.VMEM((rows, chans), BF16),
+            pltpu.VMEM((n_dp, sum_rows, padded), F32),
+            pltpu.VMEM((sum_rows, padded), F32),
+            pltpu.VMEM((n_fsdp, sum_rows, chunk), F32),
+            pltpu.VMEM((sum_rows, padded), F32),
+            dma((5, n_fsdp)),
+            dma((n_fsdp, n_dp)),
+            dma((n_fsdp,)),
+            dma((n_fsdp,)),
+            dma((n_fsdp,)),
+            dma((n_fsdp,)),
+            dma((n_dp,)),
+            dma((n_dp,)),
+            dma((n_fsdp,)),
+            dma((n_fsdp,)),
+            dma((n_fsdp,)),
+            dma((n_fsdp,)),
+        ],
+        compiler_params=pltpu.CompilerParams(
+            collective_id=0, has_side_effects=True, vmem_limit_bytes=56 * 1024 * 1024
+        ),
+        name="fused_module",
+    )(
+        frame_counts,
+        glu_input,
+        send_rows,
+        owner_rows,
+        depth_kernel,
+        norm_gain.reshape(1, chans),
+        norm_bias.reshape(1, chans),
+        point_weight,
+        cotangent,
+    )
 
 
 def conv_module(glu_rows, counts, kernel, gain_vec, bias_vec):
@@ -99,6 +568,15 @@
         P(("fsdp", "dp"), None),
     )
     out_specs = (P(("fsdp", "dp"), None), P(("fsdp", "dp"), None), P(), P())
+    n_fsdp, n_dp = mesh.shape["fsdp"], mesh.shape["dp"]
+
+    def local(*args):
+        slots = args[2].shape[1] // n_fsdp
+        panel = args[7].shape[0]
+        if slots % 16 == 0 and panel % 16 == 0 and n_fsdp % 2 == 0 and n_dp == 4:
+            return fused_call(n_fsdp, n_dp, *args)
+        return per_device(*args)
+
     return jax.shard_map(
-        per_device, mesh=mesh, in_specs=in_specs, out_specs=out_specs, check_vma=False
+        local, mesh=mesh, in_specs=in_specs, out_specs=out_specs, check_vma=False
     )

time: 185 us -> 84.9 us (0.46)
  waiting for transfers between devices: 78.6 us -> 0 us
  Pallas kernels: 0 us -> 75.6 us
  blocking collectives: 41.2 us -> 0 us
  other arithmetic: 16.3 us -> 0 us
  between operations: 14.3 us -> 0.64 us
  starting transfers between devices: 11.2 us -> 0 us
  matrix products: 8.56 us -> 0 us
  local copies, waits for them, and re-layouts: 13.8 us -> 8.31 us
    pallas_call x0 -> x1, Pallas kernels: none -> 75.6 us  [fused_call(): pl.pallas_call(functools.partial(fused_kernel, n_fsdp, n_dp), out_shape=(...]
    all_gather x1 -> x0, waiting for transfers between devices: 47.4 us -> none  [per_device(): lax.all_gather(point_weight, 'fsdp', axis=0, tiled=True)]
    psum x1 -> x0, blocking collectives: 41.2 us -> none  [per_device(): lax.psum((kernel_part, jnp.stack([gain_part, bias_part])), ('fsdp', 'dp'))]
    all_to_all x2 -> x0, waiting for transfers between devices: 30.5 us -> none  [the longest x1 30.5 us: per_device(): lax.all_to_all(parked, 'fsdp', split_axis=0, concat_axis=0, tiled=True)]
    all_to_all x2 -> x0, starting transfers between devices: 11.1 us -> none  [the longest x1 7.28 us: per_device(): lax.all_to_all(parked, 'fsdp', split_axis=0, concat_axis=0, tiled=True)]
    dot_general x2 -> x0, matrix products: 8.56 us -> none  [the longest x1 4.67 us: per_device(): lax.dot_general(home_rows, lax.all_gather(point_weight, 'fsdp', axis=0, t...]
    scatter x2 -> x0, local copies, waits for them, and re-layouts: 6.25 us -> none  [the longest x1 3.38 us: per_device(): jnp.zeros((row_count + 1, out_count), jnp.bfloat16).at[send_slot]]
    reduce_sum x5 -> x0, other arithmetic: 4.65 us -> none  [the longest x1 2.35 us: conv_module(): jnp.where(same_utt[:, None], padded[offset:offset + row_count], 0.0)]
  transfers between devices with their start and end apart: 3 -> 0, of which waited for: 2 -> 0; matrix products, arithmetic and copies ran while one was open for 15% -> 0% of each run, Pallas kernels for 0% -> 0%
where the time goes in v1:
time: 84.9 us; the launch traced here: 84.6 us
  Pallas kernels  75.6 us (89%)
  local copies, waits for them, and re-layouts  8.31 us (10%)
    pallas_call x1, Pallas kernels, fused_call(): pl.pallas_call(functools.partial(fused_kernel, n_fsdp, n_dp), out_shape=(...  75.6 us
    unnamed x8, local copies, waits for them, and re-layouts  5.72 us

profile of v1, /device:TPU:0, one launch (start us, length us, event | category | flops | bytes accessed | tf_op | source)
XLA Modules:
  0.0 84.6 jit_solution(14432796175352516012)
XLA Ops:
  0.6 1.3 %reshape.14.gain_ref = f32[1,1536]{1,0:T(1,128)} reshape(f32[1536]{0:T(1024)} %param.14) | data formatting | bytes 12288 | tf_op jit(solution)/shard_map/reshape | solution.py:473
  1.9 1.3 %reshape.15.bias_ref = f32[1,1536]{1,0:T(1,128)} reshape(f32[1536]{0:T(1024)} %param.15) | data formatting | bytes 12288 | tf_op jit(solution)/shard_map/reshape | solution.py:474
  3.2 75.6 %fused_module.1 = (bf16[160,1536]{1,0:T(8,128)(2,1)}, bf16[256,3072]{1,0:T(8,128)(2,1)}, f32[5,1536]{1,0:T(8,128)}, f32[2,1536]{1,0:T(2,128)}) custom-call(s32[1,8]{1,0:T(1,128)} %counts_ref.1, bf16[256,3072]{1,0:T(8,128)(2,1)} %glu_ref.1, s32[1,256]{1,0:T(1,128)} %send_ref.1, s32[1,160]{1,0:T(1,128)} %owner_ref.1, f32[5,1536]{1,0:T(8,128)} %taps_ref.1, ...), custom_call_target="tpu_custom_call" | custom-call | tf_op jit(solution)/shard_map/fused_module/pallas_call | solution.py:424
  78.9 1.8 %copy.17 = bf16[160,1536]{1,0:T(8,128)(2,1)} copy(bf16[160,1536]{1,0:T(8,128)(2,1)} %get-tuple-element.8) | data formatting | bytes 983040
  80.7 0.0 copy-start
  80.7 0.0 copy-start.1
  80.7 2.7 %copy.18 = bf16[256,3072]{1,0:T(8,128)(2,1)} copy(bf16[256,3072]{1,0:T(8,128)(2,1)} %get-tuple-element.9) | data formatting | bytes 3145728
  83.4 0.0 copy-done
  83.4 0.6 copy.19
  84.0 0.0 copy-done.1
  84.0 0.6 copy.20
Async XLA Ops:
  80.7 2.7 %copy-start = (f32[5,1536]{1,0:T(8,128)S(1)}, f32[5,1536]{1,0:T(8,128)}, u32[]{:S(2)}) copy-start(f32[5,1536]{1,0:T(8,128)} %get-tuple-element.10) | copy-start | bytes 92164
  80.7 3.3 %copy-start.1 = (f32[2,1536]{1,0:T(2,128)S(1)}, f32[2,1536]{1,0:T(2,128)}, u32[]{:S(2)}) copy-start(f32[2,1536]{1,0:T(2,128)} %get-tuple-element.11) | copy-start | bytes 36868

commit v2 on v1

--- a/solution.py
+++ b/solution.py
@@ -10,8 +10,30 @@
 
 eps = 1e-05
 LANES = 128
+COPY_PARTS = 2
 F32 = jnp.float32
 BF16 = jnp.bfloat16
+
+
+def sigmoid(x):
+    return 0.5 * jnp.tanh(0.5 * x) + 0.5
+
+
+def copy_kernel(*refs):
+    sources, targets, sems = refs[:4], refs[4:8], refs[8]
+    copies = []
+    for i, (source, target) in enumerate(zip(sources, targets)):
+        size = source.shape[0]
+        parts = COPY_PARTS if size % (16 * COPY_PARTS) == 0 else 1
+        step = size // parts
+        for k in range(parts):
+            at = pl.ds(k * step, step)
+            src, dst = (source, target) if parts == 1 else (source.at[at], target.at[at])
+            copies.append(pltpu.make_async_copy(src, dst, sems.at[i, k]))
+    for copy in copies:
+        copy.start()
+    for copy in copies:
+        copy.wait()
 
 
 def fused_kernel(
@@ -150,7 +172,6 @@
         lax.broadcasted_iota(jnp.int32, (rows, owned), 0) == owner_ref[...]
     ).astype(F32).astype(BF16)
     parked[...] = jnp.dot(park, cot_ref[...], preferred_element_type=F32).astype(BF16)
-    cot_copies = exchange(parked, returned, cot_send, cot_recv)
 
     w_buf[rows_of(f, panel), :] = weight_ref[...]
 
@@ -185,7 +206,7 @@
     def conv_step(i, acc):
         a = glu_ref[:, lanes_of(i)].astype(F32)
         b = glu_ref[:, pl.ds(pl.multiple_of(chans + i * LANES, LANES), LANES)].astype(F32)
-        mixed = a * jax.nn.sigmoid(b) * live_f
+        mixed = a * sigmoid(b) * live_f
         mixed_buf[:, lanes_of(i)] = mixed
         conv = jnp.zeros((rows, LANES), F32)
         for j in range(taps):
@@ -194,7 +215,16 @@
         return acc + conv
 
     zero_acc = jnp.zeros((rows, LANES), F32)
-    acc = lax.fori_loop(0, n_chunks, conv_step, zero_acc)
+    def forward_y(k):
+        p = (y_peer + 2 * k) % n_fsdp
+        wait_piece(p, d)
+        src = piece_of(p, d)
+        send_piece(src, p, d, 2, n_fsdp // 2 + k, {"fsdp": f, "dp": x_peer})
+        send_piece(src, p, d, 3, n_fsdp // 2 + k, {"fsdp": f, "dp": core_peer})
+
+    acc = lax.fori_loop(0, n_chunks // 2, conv_step, zero_acc)
+    forward_y(0)
+    acc = lax.fori_loop(n_chunks // 2, n_chunks, conv_step, acc)
     mean = jnp.sum(acc, axis=1, keepdims=True) * (1.0 / chans)
 
     for k in z_steps:
@@ -205,6 +235,8 @@
         send_piece(src, p, d, 2, k, {"fsdp": f, "dp": x_peer})
         send_piece(src, p, d, 3, k, {"fsdp": f, "dp": core_peer})
 
+    cot_copies = exchange(parked, returned, cot_send, cot_recv)
+
     def var_step(i, acc):
         diff = conv_buf[:, lanes_of(i)] - mean
         return acc + diff * diff
@@ -215,8 +247,8 @@
     def act_step(i, carry):
         xhat = (conv_buf[:, lanes_of(i)] - mean) * rstd
         conv_buf[:, lanes_of(i)] = xhat
-        normed = xhat * gain_ref[:, lanes_of(i)] + bias_ref[:, lanes_of(i)]
-        acts[:, lanes_of(i)] = (normed * jax.nn.sigmoid(normed) * live_f).astype(BF16)
+        normed = xhat * gain_ref[lanes_of(i)][None, :] + bias_ref[lanes_of(i)][None, :]
+        acts[:, lanes_of(i)] = (normed * sigmoid(normed) * live_f).astype(BF16)
         return carry
 
     lax.fori_loop(0, n_chunks, act_step, 0)
@@ -227,47 +259,42 @@
         pick, acts[...], (((0,), (0,)), ((), ())), preferred_element_type=F32
     ).astype(BF16)
 
-    for k in range(n_fsdp // 2):
-        p = (y_peer + 2 * k) % n_fsdp
-        wait_piece(p, d)
-        src = piece_of(p, d)
-        send_piece(src, p, d, 2, n_fsdp // 2 + k, {"fsdp": f, "dp": x_peer})
-        send_piece(src, p, d, 3, n_fsdp // 2 + k, {"fsdp": f, "dp": core_peer})
-
-    act_copies = exchange(outgoing, arrived, act_send, act_recv)
-
-    order = [(f + 2 * k) % n_fsdp for k in z_steps]
-    order += [(y_peer + 2 * k) % n_fsdp for k in range(n_fsdp // 2)]
-    for k, p in enumerate(order):
+    for k in z_steps:
+        forward_y(k)
+
+    order = [((y_peer + 2 * k) % n_fsdp, n_fsdp // 2 + k) for k in range(1)]
+    order += [((f + 2 * k) % n_fsdp, k) for k in z_steps]
+    order += [((y_peer + 2 * k) % n_fsdp, n_fsdp // 2 + k) for k in z_steps]
+    for p, k in order:
         wait_piece(p, x_peer)
         send_piece(piece_of(p, x_peer), p, x_peer, 4, k, {"fsdp": f, "dp": core_peer})
 
     finish_exchange(cot_copies, parked, returned, cot_send, cot_recv)
+    act_copies = exchange(outgoing, arrived, act_send, act_recv)
     home[...] = jnp.dot(pick, returned[...], preferred_element_type=F32).astype(BF16)
 
-    for p in order:
-        wait_piece(p, core_peer)
-        wait_piece(p, (core_peer + n_dp // 2) % n_dp)
-
     wide = 2 * LANES
 
-    def back_step(i, carry):
-        at = pl.ds(pl.multiple_of(i * wide, wide), wide)
+    for k in range(n_fsdp // 2):
+        arrivals = [(y_peer + 2 * k) % n_fsdp]
+        if k > 0:
+            arrivals.append((f + 2 * k) % n_fsdp)
+        for p in arrivals:
+            wait_piece(p, core_peer)
+            wait_piece(p, (core_peer + n_dp // 2) % n_dp)
+        at = rows_of((f // 2 + k) % (n_fsdp // 2), 2 * panel)
         back_buf[:, at] = lax.dot_general(
             home[...], w_buf[at, :], (((1,), (1,)), ((), ())), preferred_element_type=F32
         ).astype(BF16)
-        return carry
-
-    lax.fori_loop(0, chans // wide, back_step, 0)
 
     part = dp_in.at[d]
     dp_in[d] = jnp.zeros(dp_in.shape[1:], F32)
 
     def norm_step(i, sums):
         xhat = conv_buf[:, lanes_of(i)]
-        gain = gain_ref[:, lanes_of(i)]
-        normed = xhat * gain + bias_ref[:, lanes_of(i)]
-        s = jax.nn.sigmoid(normed)
+        gain = gain_ref[lanes_of(i)][None, :]
+        normed = xhat * gain + bias_ref[lanes_of(i)][None, :]
+        s = sigmoid(normed)
         g = back_buf[:, lanes_of(i)].astype(F32) * live_f
         dn = g * (s + normed * s * (1.0 - s))
         dnx = dn * xhat
@@ -288,12 +315,7 @@
             moved = masks[taps - 1 - j] * shifted(dconv, half - j)
             part[j : j + 1, lanes_of(i)] = jnp.sum(mixed * moved, axis=0, keepdims=True)
             dmixed = dmixed + moved * taps_ref[j : j + 1, lanes_of(i)]
-        a = glu_ref[:, lanes_of(i)].astype(F32)
-        right = pl.ds(pl.multiple_of(chans + i * LANES, LANES), LANES)
-        sb = jax.nn.sigmoid(glu_ref[:, right].astype(F32))
-        ds = dmixed * sb
-        igrad_ref[:, lanes_of(i)] = ds.astype(BF16)
-        igrad_ref[:, right] = (ds * a * (1.0 - sb)).astype(BF16)
+        grad_buf[:, lanes_of(i)] = dmixed
         return carry
 
     lax.fori_loop(0, n_chunks, grad_step, 0)
@@ -311,11 +333,16 @@
         copy.start()
         dp_copies.append(copy)
 
-    finish_exchange(act_copies, outgoing, arrived, act_send, act_recv)
-    outgoing_rows = lax.dot_general(
-        park, arrived[...], (((0,), (0,)), ((), ())), preferred_element_type=F32
-    ).astype(BF16)
-    acts[0:owned, :] = outgoing_rows
+    def input_step(i, carry):
+        a = glu_ref[:, lanes_of(i)].astype(F32)
+        right = pl.ds(pl.multiple_of(chans + i * LANES, LANES), LANES)
+        sb = sigmoid(glu_ref[:, right].astype(F32))
+        ds = grad_buf[:, lanes_of(i)] * sb
+        igrad_ref[:, lanes_of(i)] = ds.astype(BF16)
+        igrad_ref[:, right] = (ds * a * (1.0 - sb)).astype(BF16)
+        return carry
+
+    lax.fori_loop(0, n_chunks, input_step, 0)
 
     for k in range(1, n_dp):
         source = (d + k) % n_dp
@@ -345,6 +372,12 @@
         copy.start()
         rs_copies.append(copy)
     rs_in[f] = rs_src[:, rows_of(f, chunk)]
+
+    finish_exchange(act_copies, outgoing, arrived, act_send, act_recv)
+    outgoing_rows = lax.dot_general(
+        park, arrived[...], (((0,), (0,)), ((), ())), preferred_element_type=F32
+    ).astype(BF16)
+    acts[0:owned, :] = outgoing_rows
 
     def out_step(i, carry):
         at = pl.ds(pl.multiple_of(i * wide, wide), wide)
@@ -421,7 +454,7 @@
     vmem = pl.BlockSpec(memory_space=pltpu.VMEM)
     smem = pl.BlockSpec(memory_space=pltpu.SMEM)
     dma = pltpu.SemaphoreType.DMA
-    return pl.pallas_call(
+    results = pl.pallas_call(
         functools.partial(fused_kernel, n_fsdp, n_dp),
         out_shape=(
             jax.ShapeDtypeStruct((owned, cols), BF16),
@@ -470,10 +503,22 @@
         send_rows,
         owner_rows,
         depth_kernel,
-        norm_gain.reshape(1, chans),
-        norm_bias.reshape(1, chans),
+        norm_gain,
+        norm_bias,
         point_weight,
         cotangent,
+    )
+    anywhere = pl.BlockSpec(memory_space=pl.ANY)
+    return tuple(
+        pl.pallas_call(
+            copy_kernel,
+            out_shape=tuple(jax.ShapeDtypeStruct(r.shape, r.dtype) for r in results),
+            in_specs=[anywhere] * 4,
+            out_specs=(anywhere,) * 4,
+            scratch_shapes=[dma((4, COPY_PARTS))],
+            compiler_params=pltpu.CompilerParams(vmem_limit_bytes=60 * 1024 * 1024),
+            name="copy_results",
+        )(*results)
     )
 
 
@@ -573,7 +618,7 @@
     def local(*args):
         slots = args[2].shape[1] // n_fsdp
         panel = args[7].shape[0]
-        if slots % 16 == 0 and panel % 16 == 0 and n_fsdp % 2 == 0 and n_dp == 4:
+        if slots % 16 == 0 and panel % 16 == 0 and n_fsdp % 2 == 0 and n_dp == 4 and panel % 64 == 0:
             return fused_call(n_fsdp, n_dp, *args)
         return per_device(*args)
 

time: 84.9 us -> 136 us (1.60)
  Pallas kernels: 75.6 us -> 135 us
  local copies, waits for them, and re-layouts: 8.31 us -> 0 us
    pallas_call x0 -> x1, Pallas kernels: none -> 65.6 us  [fused_call(): pl.pallas_call(copy_kernel, out_shape=tuple((jax.ShapeDtypeStruct(r.shape...]
    pallas_call x1, Pallas kernels: 75.6 us -> 69.2 us  [fused_call(): pl.pallas_call(functools.partial(fused_kernel, n_fsdp, n_dp), out_shape=(...]
    unnamed x8 -> x0, local copies, waits for them, and re-layouts: 5.72 us -> none
    reshape x2 -> x0, local copies, waits for them, and re-layouts: 2.59 us -> none  [the longest x1 1.3 us: fused_call(): norm_gain.reshape(1, chans)]
where the time goes in v2:
time: 136 us; the launch traced here: 135 us
  Pallas kernels  135 us (99%)
    pallas_call x1, Pallas kernels, fused_call(): pl.pallas_call(functools.partial(fused_kernel, n_fsdp, n_dp), out_shape=(...  69.2 us
    pallas_call x1, Pallas kernels, fused_call(): pl.pallas_call(copy_kernel, out_shape=tuple((jax.ShapeDtypeStruct(r.shape...  65.6 us

profile of v2, /device:TPU:0, one launch (start us, length us, event | category | flops | bytes accessed | tf_op | source)
XLA Modules:
  0.0 135.4 jit_solution(2319611582439770479)
XLA Ops:
  0.6 69.2 %fused_module.1 = (bf16[160,1536]{1,0:T(8,128)(2,1)}, bf16[256,3072]{1,0:T(8,128)(2,1)}, f32[5,1536]{1,0:T(8,128)}, f32[2,1536]{1,0:T(2,128)}) custom-call(s32[1,8]{1,0:T(1,128)} %counts_ref.1, bf16[256,3072]{1,0:T(8,128)(2,1)} %glu_ref.1, s32[1,256]{1,0:T(1,128)} %send_ref.1, s32[1,160]{1,0:T(1,128)} %owner_ref.1, f32[5,1536]{1,0:T(8,128)} %taps_ref.1, ...), custom_call_target="tpu_custom_call" | custom-call | tf_op jit(solution)/shard_map/fused_module/pallas_call | solution.py:457
  69.8 65.6 %copy_results.1 = (bf16[160,1536]{1,0:T(8,128)(2,1)}, bf16[256,3072]{1,0:T(8,128)(2,1)}, f32[5,1536]{1,0:T(8,128)}, f32[2,1536]{1,0:T(2,128)}) custom-call(bf16[160,1536]{1,0:T(8,128)(2,1)} %get-tuple-element.8.refs_0_, bf16[256,3072]{1,0:T(8,128)(2,1)} %get-tuple-element.9.refs_1_, f32[5,1536]{1,0:T(8,128)} %get-tuple-element.10.refs_2_, ...), custom_call_target="tpu_custom_call" | custom-call | tf_op jit(solution)/shard_map/copy_results/pallas_call | solution.py:513

commit v3 on v2

--- a/solution.py
+++ b/solution.py
@@ -20,20 +20,24 @@
 
 
 def copy_kernel(*refs):
-    sources, targets, sems = refs[:4], refs[4:8], refs[8]
-    copies = []
-    for i, (source, target) in enumerate(zip(sources, targets)):
+    sources, targets, stages, in_sems, out_sems = refs[:4], refs[4:8], refs[8:12], refs[12], refs[13]
+    loads, stores = [], []
+    for i, (source, target, stage) in enumerate(zip(sources, targets, stages)):
         size = source.shape[0]
         parts = COPY_PARTS if size % (16 * COPY_PARTS) == 0 else 1
         step = size // parts
         for k in range(parts):
             at = pl.ds(k * step, step)
-            src, dst = (source, target) if parts == 1 else (source.at[at], target.at[at])
-            copies.append(pltpu.make_async_copy(src, dst, sems.at[i, k]))
-    for copy in copies:
-        copy.start()
-    for copy in copies:
-        copy.wait()
+            src, mid, dst = (r if parts == 1 else r.at[at] for r in (source, stage, target))
+            loads.append(pltpu.make_async_copy(src, mid, in_sems.at[i, k]))
+            stores.append(pltpu.make_async_copy(mid, dst, out_sems.at[i, k]))
+    for load in loads:
+        load.start()
+    for load, store in zip(loads, stores):
+        load.wait()
+        store.start()
+    for store in stores:
+        store.wait()
 
 
 def fused_kernel(
@@ -113,17 +117,24 @@
         return w_buf.at[rows_of(p, panel), rows_of(q, piece)]
 
     pending = []
-
-    def send_piece(src, p, q, kind, slot, target):
-        copy = pltpu.make_async_remote_copy(
+    zi = f // 2
+    n_z = n_fsdp // 2
+    up, down = {"fsdp": (f + 2) % n_fsdp, "dp": d}, {"fsdp": (f + n_fsdp - 2) % n_fsdp, "dp": d}
+    to_y, to_x, to_core = (
+        {"fsdp": y_peer, "dp": d},
+        {"fsdp": f, "dp": x_peer},
+        {"fsdp": f, "dp": core_peer},
+    )
+    can_up, can_down = zi + 1 < n_z, zi >= 1
+
+    def piece_copy(src, p, q, kind, target):
+        return pltpu.make_async_remote_copy(
             src_ref=src,
             dst_ref=piece_of(p, q),
-            send_sem=w_send.at[kind, slot],
+            send_sem=w_send.at[kind, p],
             recv_sem=w_recv.at[p, q],
             device_id=target,
         )
-        copy.start()
-        pending.append(copy)
 
     def wait_piece(p, q):
         pltpu.make_async_remote_copy(
@@ -135,10 +146,89 @@
         ).wait_recv()
 
     own_piece = weight_ref.at[:, rows_of(d, piece)]
-    z_steps = range(1, n_fsdp // 2)
-    for k in z_steps:
-        send_piece(own_piece, f, d, 0, k, {"fsdp": (f + 2 * k) % n_fsdp, "dp": d})
-    send_piece(own_piece, f, d, 1, 0, {"fsdp": y_peer, "dp": d})
+
+    @pl.when(can_up)
+    def _():
+        piece_copy(own_piece, f, d, 0, up).start()
+
+    @pl.when(can_down)
+    def _():
+        piece_copy(own_piece, f, d, 1, down).start()
+
+    piece_copy(own_piece, f, d, 2, to_y).start()
+
+    def each_side(step, base, body):
+        if step == 0:
+            body(base, None)
+            return
+
+        @pl.when(zi >= step)
+        def _():
+            body((base + n_fsdp - 2 * step) % n_fsdp, True)
+
+        @pl.when(zi + step < n_z)
+        def _():
+            body((base + 2 * step) % n_fsdp, False)
+
+    def spread(p):
+        piece_copy(piece_of(p, d), p, d, 3, to_x).start()
+        piece_copy(piece_of(p, d), p, d, 4, to_core).start()
+
+    def forward_z(step):
+        def body(p, rising):
+            wait_piece(p, d)
+            src = piece_of(p, d)
+
+            @pl.when(can_up if rising else can_down)
+            def _():
+                piece_copy(src, p, d, 0 if rising else 1, up if rising else down).start()
+
+            piece_copy(src, p, d, 2, to_y).start()
+            spread(p)
+
+        each_side(step, f, body)
+
+    def forward_y(step):
+        def body(p, rising):
+            wait_piece(p, d)
+            spread(p)
+
+        each_side(step, y_peer, body)
+
+    def forward_x(step):
+        def body(p, rising):
+            wait_piece(p, x_peer)
+            piece_copy(piece_of(p, x_peer), p, x_peer, 5, to_core).start()
+
+        if step > 0:
+            each_side(step, f, body)
+        each_side(step, y_peer, body)
+
+    def finish_pieces():
+        def moved(p, rising):
+            piece_copy(piece_of(p, d), p, d, 2, to_y).wait_send()
+
+            @pl.when(can_up if rising else can_down)
+            def _():
+                piece_copy(piece_of(p, d), p, d, 0 if rising else 1, up if rising else down).wait_send()
+
+        for step in range(1, n_z):
+            each_side(step, f, moved)
+
+        @pl.when(can_up)
+        def _():
+            piece_copy(own_piece, f, d, 0, up).wait_send()
+
+        @pl.when(can_down)
+        def _():
+            piece_copy(own_piece, f, d, 1, down).wait_send()
+
+        piece_copy(own_piece, f, d, 2, to_y).wait_send()
+        for k in range(1, n_fsdp):
+            p = (f + k) % n_fsdp
+            piece_copy(piece_of(p, d), p, d, 3, to_x).wait_send()
+            piece_copy(piece_of(p, d), p, d, 4, to_core).wait_send()
+            piece_copy(piece_of(p, x_peer), p, x_peer, 5, to_core).wait_send()
 
     def exchange(src, dst, send_sem, recv_sem):
         copies = []
@@ -215,26 +305,14 @@
         return acc + conv
 
     zero_acc = jnp.zeros((rows, LANES), F32)
-    def forward_y(k):
-        p = (y_peer + 2 * k) % n_fsdp
-        wait_piece(p, d)
-        src = piece_of(p, d)
-        send_piece(src, p, d, 2, n_fsdp // 2 + k, {"fsdp": f, "dp": x_peer})
-        send_piece(src, p, d, 3, n_fsdp // 2 + k, {"fsdp": f, "dp": core_peer})
-
     acc = lax.fori_loop(0, n_chunks // 2, conv_step, zero_acc)
+    forward_z(1)
     forward_y(0)
     acc = lax.fori_loop(n_chunks // 2, n_chunks, conv_step, acc)
     mean = jnp.sum(acc, axis=1, keepdims=True) * (1.0 / chans)
 
-    for k in z_steps:
-        p = (f + 2 * k) % n_fsdp
-        wait_piece(p, d)
-        src = piece_of(p, d)
-        send_piece(src, p, d, 1, k, {"fsdp": y_peer, "dp": d})
-        send_piece(src, p, d, 2, k, {"fsdp": f, "dp": x_peer})
-        send_piece(src, p, d, 3, k, {"fsdp": f, "dp": core_peer})
-
+    forward_z(2)
+    forward_y(1)
     cot_copies = exchange(parked, returned, cot_send, cot_recv)
 
     def var_step(i, acc):
@@ -243,6 +321,10 @@
 
     acc = lax.fori_loop(0, n_chunks, var_step, zero_acc)
     rstd = lax.rsqrt(jnp.sum(acc, axis=1, keepdims=True) * (1.0 / chans) + eps)
+
+    for step in range(3, n_z):
+        forward_z(step)
+    forward_y(2)
 
     def act_step(i, carry):
         xhat = (conv_buf[:, lanes_of(i)] - mean) * rstd
@@ -259,15 +341,10 @@
         pick, acts[...], (((0,), (0,)), ((), ())), preferred_element_type=F32
     ).astype(BF16)
 
-    for k in z_steps:
-        forward_y(k)
-
-    order = [((y_peer + 2 * k) % n_fsdp, n_fsdp // 2 + k) for k in range(1)]
-    order += [((f + 2 * k) % n_fsdp, k) for k in z_steps]
-    order += [((y_peer + 2 * k) % n_fsdp, n_fsdp // 2 + k) for k in z_steps]
-    for p, k in order:
-        wait_piece(p, x_peer)
-        send_piece(piece_of(p, x_peer), p, x_peer, 4, k, {"fsdp": f, "dp": core_peer})
+    for step in range(3, n_z):
+        forward_y(step)
+    for step in range(n_z):
+        forward_x(step)
 
     finish_exchange(cot_copies, parked, returned, cot_send, cot_recv)
     act_copies = exchange(outgoing, arrived, act_send, act_recv)
@@ -275,17 +352,24 @@
 
     wide = 2 * LANES
 
-    for k in range(n_fsdp // 2):
-        arrivals = [(y_peer + 2 * k) % n_fsdp]
-        if k > 0:
-            arrivals.append((f + 2 * k) % n_fsdp)
-        for p in arrivals:
+    def back_part(step):
+        def wait_core(p):
             wait_piece(p, core_peer)
             wait_piece(p, (core_peer + n_dp // 2) % n_dp)
-        at = rows_of((f // 2 + k) % (n_fsdp // 2), 2 * panel)
-        back_buf[:, at] = lax.dot_general(
-            home[...], w_buf[at, :], (((1,), (1,)), ((), ())), preferred_element_type=F32
-        ).astype(BF16)
+
+        def body(p, rising):
+            wait_core(p + 1 - 2 * (p % 2))
+            if step > 0:
+                wait_core(p)
+            at = rows_of(p // 2, 2 * panel)
+            back_buf[:, at] = lax.dot_general(
+                home[...], w_buf[at, :], (((1,), (1,)), ((), ())), preferred_element_type=F32
+            ).astype(BF16)
+
+        each_side(step, f, body)
+
+    for step in range(n_z):
+        back_part(step)
 
     part = dp_in.at[d]
     dp_in[d] = jnp.zeros(dp_in.shape[1:], F32)
@@ -427,6 +511,7 @@
     pending.extend(ag_copies)
     kgrad_ref[...] = full[0:taps, 0:chans]
     ngrad_ref[...] = full[taps : taps + 2, 0:chans]
+    finish_pieces()
     for copy in pending:
         copy.wait_send()
 
@@ -480,7 +565,7 @@
             pltpu.VMEM((sum_rows, padded), F32),
             pltpu.VMEM((n_fsdp, sum_rows, chunk), F32),
             pltpu.VMEM((sum_rows, padded), F32),
-            dma((5, n_fsdp)),
+            dma((6, n_fsdp)),
             dma((n_fsdp, n_dp)),
             dma((n_fsdp,)),
             dma((n_fsdp,)),
@@ -515,7 +600,8 @@
             out_shape=tuple(jax.ShapeDtypeStruct(r.shape, r.dtype) for r in results),
             in_specs=[anywhere] * 4,
             out_specs=(anywhere,) * 4,
-            scratch_shapes=[dma((4, COPY_PARTS))],
+            scratch_shapes=[pltpu.VMEM(r.shape, r.dtype) for r in results]
+            + [dma((4, COPY_PARTS))] * 2,
             compiler_params=pltpu.CompilerParams(vmem_limit_bytes=60 * 1024 * 1024),
             name="copy_results",
         )(*results)
@@ -618,7 +704,7 @@
     def local(*args):
         slots = args[2].shape[1] // n_fsdp
         panel = args[7].shape[0]
-        if slots % 16 == 0 and panel % 16 == 0 and n_fsdp % 2 == 0 and n_dp == 4 and panel % 64 == 0:
+        if slots % 16 == 0 and panel % 16 == 0 and n_fsdp % 2 == 0 and n_fsdp >= 6 and n_dp == 4 and panel % 64 == 0:
             return fused_call(n_fsdp, n_dp, *args)
         return per_device(*args)
 

time: 136 us -> 67.9 us (0.50)
  Pallas kernels: 135 us -> 67 us
    pallas_call x1, Pallas kernels: 65.6 us -> 2.67 us  [fused_call(): pl.pallas_call(copy_kernel, out_shape=tuple((jax.ShapeDtypeStruct(r.shape...]
    pallas_call x1, Pallas kernels: 69.2 us -> 64.4 us  [fused_call(): pl.pallas_call(functools.partial(fused_kernel, n_fsdp, n_dp), out_shape=(...]
where the time goes in v3:
time: 67.9 us; the launch traced here: 67.7 us
  Pallas kernels  67 us (99%)
    pallas_call x1, Pallas kernels, fused_call(): pl.pallas_call(functools.partial(fused_kernel, n_fsdp, n_dp), out_shape=(...  64.4 us
    pallas_call x1, Pallas kernels, fused_call(): pl.pallas_call(copy_kernel, out_shape=tuple((jax.ShapeDtypeStruct(r.shape...  2.67 us

profile of v3, /device:TPU:0, one launch (start us, length us, event | category | flops | bytes accessed | tf_op | source)
XLA Modules:
  0.0 67.7 jit_solution(12894938421411625232)
XLA Ops:
  0.6 64.4 %fused_module.1 = (bf16[160,1536]{1,0:T(8,128)(2,1)}, bf16[256,3072]{1,0:T(8,128)(2,1)}, f32[5,1536]{1,0:T(8,128)}, f32[2,1536]{1,0:T(2,128)}) custom-call(s32[1,8]{1,0:T(1,128)} %counts_ref.1, bf16[256,3072]{1,0:T(8,128)(2,1)} %glu_ref.1, s32[1,256]{1,0:T(1,128)} %send_ref.1, s32[1,160]{1,0:T(1,128)} %owner_ref.1, f32[5,1536]{1,0:T(8,128)} %taps_ref.1, ...), custom_call_target="tpu_custom_call" | custom-call | tf_op jit(solution)/shard_map/fused_module/pallas_call | solution.py:542
  65.0 2.7 %copy_results.1 = (bf16[160,1536]{1,0:T(8,128)(2,1)}, bf16[256,3072]{1,0:T(8,128)(2,1)}, f32[5,1536]{1,0:T(8,128)}, f32[2,1536]{1,0:T(2,128)}) custom-call(bf16[160,1536]{1,0:T(8,128)(2,1)} %get-tuple-element.8.refs_0_, bf16[256,3072]{1,0:T(8,128)(2,1)} %get-tuple-element.9.refs_1_, f32[5,1536]{1,0:T(8,128)} %get-tuple-element.10.refs_2_, ...), custom_call_target="tpu_custom_call" | custom-call | tf_op jit(solution)/shard_map/copy_results/pallas_call | solution.py:598

commit v4 on v3

--- a/solution.py
+++ b/solution.py
@@ -44,18 +44,23 @@
     n_fsdp,
     n_dp,
     counts_ref,
-    glu_ref,
+    glu_hbm,
     send_ref,
     owner_ref,
     taps_ref,
     gain_ref,
     bias_ref,
     weight_ref,
-    cot_ref,
+    cot_hbm,
     out_ref,
-    igrad_ref,
+    igrad_hbm,
     kgrad_ref,
     ngrad_ref,
+    glu_ref,
+    cot_ref,
+    igrad_ref,
+    shift_buf,
+    io_sems,
     w_buf,
     parked,
     returned,
@@ -103,6 +108,15 @@
     x_peer = (d + n_dp // 2) % n_dp
     core_peer = d + 1 - 2 * (d % 2)
 
+    panel_rows = pl.ds(pl.multiple_of(f * panel, panel), panel)
+    cot_load = pltpu.make_async_copy(cot_hbm, cot_ref, io_sems.at[0])
+    glu_load = pltpu.make_async_copy(glu_hbm, glu_ref, io_sems.at[1])
+    panel_load = pltpu.make_async_copy(weight_ref, w_buf.at[panel_rows], io_sems.at[2])
+    cot_load.start()
+    glu_load.start()
+    panel_load.start()
+    shift_buf[...] = jnp.zeros_like(shift_buf)
+
     barrier = pltpu.get_barrier_semaphore()
     for k in range(1, n_fsdp):
         pl.semaphore_signal(barrier, inc=1, device_id={"fsdp": (f + k) % n_fsdp, "dp": d})
@@ -261,9 +275,11 @@
     park = (
         lax.broadcasted_iota(jnp.int32, (rows, owned), 0) == owner_ref[...]
     ).astype(F32).astype(BF16)
+    cot_load.wait()
     parked[...] = jnp.dot(park, cot_ref[...], preferred_element_type=F32).astype(BF16)
 
-    w_buf[rows_of(f, panel), :] = weight_ref[...]
+    glu_load.wait()
+    panel_load.wait()
 
     ends = []
     total = jnp.int32(0)
@@ -290,17 +306,20 @@
     def lanes_of(i):
         return pl.ds(pl.multiple_of(i * LANES, LANES), LANES)
 
-    def shifted(x, offset):
-        return x if offset == 0 else pltpu.roll(x, (-offset) % rows, 0)
+    def shifted(x, mask, offset):
+        if offset == 0:
+            return x
+        return mask * shift_buf[8 + offset : 8 + offset + rows, :]
 
     def conv_step(i, acc):
         a = glu_ref[:, lanes_of(i)].astype(F32)
         b = glu_ref[:, pl.ds(pl.multiple_of(chans + i * LANES, LANES), LANES)].astype(F32)
         mixed = a * sigmoid(b) * live_f
         mixed_buf[:, lanes_of(i)] = mixed
+        shift_buf[8 : 8 + rows, :] = mixed
         conv = jnp.zeros((rows, LANES), F32)
         for j in range(taps):
-            conv = conv + masks[j] * shifted(mixed, j - half) * taps_ref[j : j + 1, lanes_of(i)]
+            conv = conv + shifted(mixed, masks[j], j - half) * taps_ref[j : j + 1, lanes_of(i)]
         conv_buf[:, lanes_of(i)] = conv
         return acc + conv
 
@@ -343,11 +362,13 @@
 
     for step in range(3, n_z):
         forward_y(step)
-    for step in range(n_z):
+    forward_x(0)
+    forward_x(1)
+    act_copies = exchange(outgoing, arrived, act_send, act_recv)
+    for step in range(2, n_z):
         forward_x(step)
 
     finish_exchange(cot_copies, parked, returned, cot_send, cot_recv)
-    act_copies = exchange(outgoing, arrived, act_send, act_recv)
     home[...] = jnp.dot(pick, returned[...], preferred_element_type=F32).astype(BF16)
 
     wide = 2 * LANES
@@ -393,10 +414,11 @@
 
     def grad_step(i, carry):
         dconv = rstd * (grad_buf[:, lanes_of(i)] - first - conv_buf[:, lanes_of(i)] * second)
+        shift_buf[8 : 8 + rows, :] = dconv
         mixed = mixed_buf[:, lanes_of(i)]
         dmixed = jnp.zeros((rows, LANES), F32)
         for j in range(taps):
-            moved = masks[taps - 1 - j] * shifted(dconv, half - j)
+            moved = shifted(dconv, masks[taps - 1 - j], half - j)
             part[j : j + 1, lanes_of(i)] = jnp.sum(mixed * moved, axis=0, keepdims=True)
             dmixed = dmixed + moved * taps_ref[j : j + 1, lanes_of(i)]
         grad_buf[:, lanes_of(i)] = dmixed
@@ -426,7 +448,7 @@
         igrad_ref[:, right] = (ds * a * (1.0 - sb)).astype(BF16)
         return carry
 
-    lax.fori_loop(0, n_chunks, input_step, 0)
+    lax.fori_loop(0, n_chunks // 2, input_step, 0)
 
     for k in range(1, n_dp):
         source = (d + k) % n_dp
@@ -457,20 +479,9 @@
         rs_copies.append(copy)
     rs_in[f] = rs_src[:, rows_of(f, chunk)]
 
-    finish_exchange(act_copies, outgoing, arrived, act_send, act_recv)
-    outgoing_rows = lax.dot_general(
-        park, arrived[...], (((0,), (0,)), ((), ())), preferred_element_type=F32
-    ).astype(BF16)
-    acts[0:owned, :] = outgoing_rows
-
-    def out_step(i, carry):
-        at = pl.ds(pl.multiple_of(i * wide, wide), wide)
-        out_ref[:, at] = jnp.dot(
-            acts[0:owned, :], w_buf[:, at], preferred_element_type=F32
-        ).astype(BF16)
-        return carry
-
-    lax.fori_loop(0, cols // wide, out_step, 0)
+    lax.fori_loop(n_chunks // 2, n_chunks, input_step, 0)
+    igrad_store = pltpu.make_async_copy(igrad_ref, igrad_hbm, io_sems.at[3])
+    igrad_store.start()
 
     for k in range(1, n_fsdp):
         source = (f + k) % n_fsdp
@@ -499,6 +510,22 @@
         )
         copy.start()
         ag_copies.append(copy)
+
+    finish_exchange(act_copies, outgoing, arrived, act_send, act_recv)
+    outgoing_rows = lax.dot_general(
+        park, arrived[...], (((0,), (0,)), ((), ())), preferred_element_type=F32
+    ).astype(BF16)
+    acts[0:owned, :] = outgoing_rows
+
+    def out_step(i, carry):
+        at = pl.ds(pl.multiple_of(i * wide, wide), wide)
+        out_ref[:, at] = jnp.dot(
+            acts[0:owned, :], w_buf[:, at], preferred_element_type=F32
+        ).astype(BF16)
+        return carry
+
+    lax.fori_loop(0, cols // wide, out_step, 0)
+
     for k in range(1, n_fsdp):
         source = (f + k) % n_fsdp
         pltpu.make_async_remote_copy(
@@ -511,6 +538,7 @@
     pending.extend(ag_copies)
     kgrad_ref[...] = full[0:taps, 0:chans]
     ngrad_ref[...] = full[taps : taps + 2, 0:chans]
+    igrad_store.wait()
     finish_pieces()
     for copy in pending:
         copy.wait_send()
@@ -537,6 +565,7 @@
     chunk = -(-chans // (n_fsdp * LANES)) * LANES
     padded = chunk * n_fsdp
     vmem = pl.BlockSpec(memory_space=pltpu.VMEM)
+    anywhere = pl.BlockSpec(memory_space=pl.ANY)
     smem = pl.BlockSpec(memory_space=pltpu.SMEM)
     dma = pltpu.SemaphoreType.DMA
     results = pl.pallas_call(
@@ -547,9 +576,14 @@
             jax.ShapeDtypeStruct((taps, chans), F32),
             jax.ShapeDtypeStruct((2, chans), F32),
         ),
-        in_specs=[smem] + [vmem] * 8,
-        out_specs=(vmem,) * 4,
+        in_specs=[smem, anywhere] + [vmem] * 5 + [anywhere] * 2,
+        out_specs=(vmem, anywhere, vmem, vmem),
         scratch_shapes=[
+            pltpu.VMEM((rows, glu_cols), BF16),
+            pltpu.VMEM((owned, cols), BF16),
+            pltpu.VMEM((rows, glu_cols), BF16),
+            pltpu.VMEM((rows + 16, LANES), F32),
+            dma((4,)),
             pltpu.VMEM((chans, cols), BF16),
             pltpu.VMEM((rows, cols), BF16),
             pltpu.VMEM((rows, cols), BF16),
@@ -593,7 +627,6 @@
         point_weight,
         cotangent,
     )
-    anywhere = pl.BlockSpec(memory_space=pl.ANY)
     return tuple(
         pl.pallas_call(
             copy_kernel,

time: 67.9 us -> 71.8 us (1.057)
  Pallas kernels: 67 us -> 70.9 us
    pallas_call x1, Pallas kernels: 64.4 us -> 68.2 us  [fused_call(): pl.pallas_call(functools.partial(fused_kernel, n_fsdp, n_dp), out_shape=(...]
where the time goes in v4:
time: 71.8 us; the launch traced here: 71.6 us
  Pallas kernels  70.9 us (99%)
    pallas_call x1, Pallas kernels, fused_call(): pl.pallas_call(functools.partial(fused_kernel, n_fsdp, n_dp), out_shape=(...  68.2 us
    pallas_call x1, Pallas kernels, fused_call(): pl.pallas_call(copy_kernel, out_shape=tuple((jax.ShapeDtypeStruct(r.shape...  2.67 us

profile of v4, /device:TPU:0, one launch (start us, length us, event | category | flops | bytes accessed | tf_op | source)
XLA Modules:
  0.0 71.6 jit_solution(11190450530598663121)
XLA Ops:
  0.6 68.2 %fused_module.1 = (bf16[160,1536]{1,0:T(8,128)(2,1)}, bf16[256,3072]{1,0:T(8,128)(2,1)}, f32[5,1536]{1,0:T(8,128)}, f32[2,1536]{1,0:T(2,128)}) custom-call(s32[1,8]{1,0:T(1,128)} %counts_ref.1, bf16[256,3072]{1,0:T(8,128)(2,1)} %glu_hbm.1, s32[1,256]{1,0:T(1,128)} %send_ref.1, s32[1,160]{1,0:T(1,128)} %owner_ref.1, f32[5,1536]{1,0:T(8,128)} %taps_ref.1, ...), custom_call_target="tpu_custom_call" | custom-call | tf_op jit(solution)/shard_map/fused_module/pallas_call | solution.py:571
  68.9 2.7 %copy_results.1 = (bf16[160,1536]{1,0:T(8,128)(2,1)}, bf16[256,3072]{1,0:T(8,128)(2,1)}, f32[5,1536]{1,0:T(8,128)}, f32[2,1536]{1,0:T(2,128)}) custom-call(bf16[160,1536]{1,0:T(8,128)(2,1)} %get-tuple-element.8.refs_0_, bf16[256,3072]{1,0:T(8,128)(2,1)} %get-tuple-element.9.refs_1_, f32[5,1536]{1,0:T(8,128)} %get-tuple-element.10.refs_2_, ...), custom_call_target="tpu_custom_call" | custom-call | tf_op jit(solution)/shard_map/copy_results/pallas_call | solution.py:631

commit v5 on v4

--- a/solution.py
+++ b/solution.py
@@ -362,13 +362,11 @@
 
     for step in range(3, n_z):
         forward_y(step)
-    forward_x(0)
-    forward_x(1)
+    for step in range(n_z):
+        forward_x(step)
+
+    finish_exchange(cot_copies, parked, returned, cot_send, cot_recv)
     act_copies = exchange(outgoing, arrived, act_send, act_recv)
-    for step in range(2, n_z):
-        forward_x(step)
-
-    finish_exchange(cot_copies, parked, returned, cot_send, cot_recv)
     home[...] = jnp.dot(pick, returned[...], preferred_element_type=F32).astype(BF16)
 
     wide = 2 * LANES

time: 71.8 us -> 66.8 us (0.930)
  Pallas kernels: 70.9 us -> 65.9 us
    pallas_call x1, Pallas kernels: 68.2 us -> 63.3 us  [fused_call(): pl.pallas_call(functools.partial(fused_kernel, n_fsdp, n_dp), out_shape=(...]
where the time goes in v5:
time: 66.8 us; the launch traced here: 66.6 us
  Pallas kernels  65.9 us (99%)
    pallas_call x1, Pallas kernels, fused_call(): pl.pallas_call(functools.partial(fused_kernel, n_fsdp, n_dp), out_shape=(...  63.3 us
    pallas_call x1, Pallas kernels, fused_call(): pl.pallas_call(copy_kernel, out_shape=tuple((jax.ShapeDtypeStruct(r.shape...  2.67 us

profile of v5, /device:TPU:0, one launch (start us, length us, event | category | flops | bytes accessed | tf_op | source)
XLA Modules:
  0.0 66.6 jit_solution(8017815788187813809)
XLA Ops:
  0.6 63.3 %fused_module.1 = (bf16[160,1536]{1,0:T(8,128)(2,1)}, bf16[256,3072]{1,0:T(8,128)(2,1)}, f32[5,1536]{1,0:T(8,128)}, f32[2,1536]{1,0:T(2,128)}) custom-call(s32[1,8]{1,0:T(1,128)} %counts_ref.1, bf16[256,3072]{1,0:T(8,128)(2,1)} %glu_hbm.1, s32[1,256]{1,0:T(1,128)} %send_ref.1, s32[1,160]{1,0:T(1,128)} %owner_ref.1, f32[5,1536]{1,0:T(8,128)} %taps_ref.1, ...), custom_call_target="tpu_custom_call" | custom-call | tf_op jit(solution)/shard_map/fused_module/pallas_call | solution.py:569
  63.9 2.7 %copy_results.1 = (bf16[160,1536]{1,0:T(8,128)(2,1)}, bf16[256,3072]{1,0:T(8,128)(2,1)}, f32[5,1536]{1,0:T(8,128)}, f32[2,1536]{1,0:T(2,128)}) custom-call(bf16[160,1536]{1,0:T(8,128)(2,1)} %get-tuple-element.8.refs_0_, bf16[256,3072]{1,0:T(8,128)(2,1)} %get-tuple-element.9.refs_1_, f32[5,1536]{1,0:T(8,128)} %get-tuple-element.10.refs_2_, ...), custom_call_target="tpu_custom_call" | custom-call | tf_op jit(solution)/shard_map/copy_results/pallas_call | solution.py:629
